TPU v7x, 32 devices: a whole 2x2x4 slice. The times are simulated.
32 devices in a mesh: dp: 2 (over y), ctx: 8 (over z, core), head: 2 (over x).
Axes of the slice: x: 2, y: 2, z: 4, core: 2. Of those that a mesh axis runs over, the one named last changes fastest.
Arguments:
- queries: bfloat16 [2, 2048, 2048], P('dp', 'ctx', 'head'), may hold values from -35 to 35
- key_rows: bfloat16 [2, 2048, 2048], P('dp', 'ctx', 'head'), may hold values from -6 to 6
- value_rows: bfloat16 [2, 2048, 2048], P('dp', 'ctx', 'head'), may hold values from -6 to 6
- sink_logits: float32 [16], P('head'), may hold values from 4 to 9
- partner: int32 [3, 8], replicated, may hold values from 0 to 7, as said below
- block_pick: int32 [2, 3, 8], P('dp'), may hold values from 0 to 1
- out_grad: bfloat16 [2, 2048, 2048], P('dp', 'ctx', 'head'), may hold values from -18 to 18
Outputs:
- attention: bfloat16 [2, 2048, 2048], P('dp', 'ctx', 'head')
- query_grad: bfloat16 [2, 2048, 2048], P('dp', 'ctx', 'head')
- key_grad: bfloat16 [2, 2048, 2048], P('dp', 'ctx', 'head')
- value_grad: bfloat16 [2, 2048, 2048], P('dp', 'ctx', 'head')
- sink_grad: float32 [16], P('head')
Inputs may be any that keep to these rules, and one draw needn't show every extreme that they name: partner[r, i] = i XOR partner[r, 0] for every round r, and partner[r, 0] is a power of two: each round pairs the indices of ctx that differ in one bit.
All inputs are finite; a program needn't handle non-finite values.
Results may differ from a plain program's by a relative error of at most 0.0093.
Values may be sent and summed in bfloat16 or wider, within the bound.
A program may use at most 128 MiB of HBM per device.

v0:
```python
import math

import jax
import jax.numpy as jnp
from jax import lax
from jax.sharding import PartitionSpec as P

HD = 128
BLOCK = 128
ROUNDS = 3


def partner_2(value, axis, apart):
    mask = 2**apart
    pairs = [(source, source ^ mask) for source in range(lax.axis_size(axis))]
    return lax.ppermute(value, axis, pairs)


def broadcast(value, axis, source):
    kept = jnp.where(lax.axis_index(axis) == source, value, 0).astype(value.dtype)
    return lax.psum(kept, axis)


def padded(shard, sides, width):
    for axis, dim in sides:
        peers, length = (lax.axis_size(axis), shard.shape[dim])
        up = [(i, (i + 1) % peers) for i in range(peers - 1)]
        down = [(j, i) for i, j in up]
        last = lax.slice_in_dim(shard, length - width, length, axis=dim)
        leading = lax.slice_in_dim(shard, 0, width, axis=dim)
        before = lax.ppermute(last, axis, up)
        after = lax.ppermute(leading, axis, down)
        shard = jnp.concatenate([before, shard, after], axis=dim)
    return shard


def passed_along(shard, axis, by):
    peers = lax.axis_size(axis)
    pairs = [(i, i + by) for i in range(peers) if 0 <= i + by < peers]
    return lax.ppermute(shard, axis, pairs)


def to_heads(matrix, head_count):
    return matrix.reshape(matrix.shape[0], head_count, HD).transpose(1, 0, 2)


def from_heads(tensor):
    return tensor.transpose(1, 0, 2).reshape(tensor.shape[1], tensor.shape[0] * tensor.shape[2])


def place_rows(piece, start, length_total):
    widths = [(0, 0)] * piece.ndim
    widths[piece.ndim - 2] = (start, length_total - start - piece.shape[-2])
    return jnp.pad(piece, widths)


def route_apart(package, xor_mask, bit_count):
    for bit_place in range(bit_count):
        arrived = partner_2(package, "ctx", bit_place)
        package = jnp.where(jnp.right_shift(xor_mask, bit_place) % 2 == 1, arrived, package)
    return package


def return_apart(package, xor_mask, bit_count):
    for bit_place in range(bit_count):
        arrived = partner_2(package, "ctx", bit_place)
        package = jnp.where(jnp.right_shift(xor_mask, bit_place) % 2 == 1, arrived, package)
    return package


def body(queries, key_rows, value_rows, sink_logits, partner, block_pick, out_grad):
    own_query = queries[0]
    own_keys = key_rows[0]
    own_values = value_rows[0]
    own_grad = out_grad[0]
    tokens = own_query.shape[0]
    feature_width = own_query.shape[1]
    head_count = feature_width // HD
    shard_blocks = tokens // BLOCK
    ctx_count = lax.axis_size("ctx")
    ctx_place = lax.axis_index("ctx")
    bit_count = ctx_count.bit_length() - 1
    scaling = HD ** (-0.5)
    is_first = ctx_place == 0
    is_last = ctx_place == ctx_count - 1
    slot_count = (5 + ROUNDS) * BLOCK
    first_pack = jnp.stack(
        [own_query[:BLOCK], own_keys[:BLOCK], own_values[:BLOCK], own_grad[:BLOCK]]
    )
    last_pack = jnp.stack(
        [
            own_query[tokens - BLOCK :],
            own_keys[tokens - BLOCK :],
            own_values[tokens - BLOCK :],
            own_grad[tokens - BLOCK :],
        ]
    )
    first_got = broadcast(first_pack, "ctx", 0)
    last_got = broadcast(last_pack, "ctx", ctx_count - 1)
    global_pack = jnp.concatenate([first_got, last_got], axis=1)
    global_query = to_heads(global_pack[0], head_count)
    global_grad = to_heads(global_pack[3], head_count)
    pair_rows = jnp.concatenate([own_keys, own_values], axis=1)
    extended = padded(pair_rows, (("ctx", 0),), BLOCK)
    xor_masks = partner[:, 0]
    partner_place = jnp.bitwise_xor(ctx_place, xor_masks)
    ctx_match = jnp.arange(ctx_count)[None, :] == partner_place[:, None]
    wanted = jnp.sum(jnp.where(ctx_match, block_pick[0], 0), axis=1)
    packages = jnp.stack(
        [
            lax.dynamic_slice_in_dim(pair_rows, wanted[number] * BLOCK, BLOCK, 0)
            for number in range(ROUNDS)
        ]
    )
    fetched = jnp.stack(
        [route_apart(packages[number], xor_masks[number], bit_count) for number in range(ROUNDS)]
    )
    global_pair = jnp.concatenate([global_pack[1], global_pack[2]], axis=1)
    shared_pair = jnp.concatenate(
        [global_pair, fetched.reshape(ROUNDS * BLOCK, 2 * feature_width)], axis=0
    )
    window_pair = jnp.stack(
        [
            extended[step * BLOCK : step * BLOCK + tokens].reshape(
                shard_blocks, BLOCK, 2 * feature_width
            )
            for step in range(3)
        ],
        axis=1,
    ).reshape(shard_blocks, 3 * BLOCK, 2 * feature_width)
    slot_pair = jnp.concatenate(
        [
            window_pair,
            jnp.broadcast_to(
                shared_pair[None], (shard_blocks, (2 + ROUNDS) * BLOCK, 2 * feature_width)
            ),
        ],
        axis=1,
    )
    slot_keys = (
        slot_pair[:, :, :feature_width]
        .reshape(shard_blocks, slot_count, head_count, HD)
        .transpose(2, 0, 1, 3)
    )
    slot_values = (
        slot_pair[:, :, feature_width:]
        .reshape(shard_blocks, slot_count, head_count, HD)
        .transpose(2, 0, 1, 3)
    )
    query_heads = to_heads(own_query, head_count)
    query_blocks = query_heads.reshape(head_count, shard_blocks, BLOCK, HD)
    key_heads = to_heads(own_keys, head_count)
    value_heads = to_heads(own_values, head_count)
    block_index = jnp.arange(shard_blocks)
    prev_ok = jnp.logical_not(is_first & (block_index == 1))
    next_ok = jnp.logical_not(is_last & (block_index == shard_blocks - 2))
    slot_valid = jnp.concatenate(
        [
            jnp.broadcast_to(prev_ok[:, None], (shard_blocks, BLOCK)),
            jnp.ones((shard_blocks, BLOCK), bool),
            jnp.broadcast_to(next_ok[:, None], (shard_blocks, BLOCK)),
            jnp.ones((shard_blocks, (2 + ROUNDS) * BLOCK), bool),
        ],
        axis=1,
    )
    sink_grid = sink_logits[:, None, None]
    scores = (
        jnp.einsum("hnqd,hnkd->hnqk", query_blocks, slot_keys, preferred_element_type=jnp.float32)
        * scaling
    )
    scores = jnp.where(slot_valid[None, :, None, :], scores, -jnp.inf)
    row_top = jnp.maximum(sink_grid, jnp.max(scores, axis=3))
    expo = jnp.exp(scores - row_top[..., None])
    row_total = jnp.exp(sink_grid - row_top) + jnp.sum(expo, axis=3)
    regular_acc = jnp.einsum(
        "hnqk,hnkd->hnqd",
        expo.astype(jnp.bfloat16),
        slot_values,
        preferred_element_type=jnp.float32,
    )
    regular_out = (regular_acc / row_total[..., None]).reshape(head_count, tokens, HD)
    regular_lse = (row_top + jnp.log(row_total)).reshape(head_count, tokens)
    global_scores = (
        jnp.einsum("hgd,htd->hgt", global_query, key_heads, preferred_element_type=jnp.float32)
        * scaling
    )
    local_top = jnp.max(global_scores, axis=2)
    global_top = jnp.maximum(lax.pmax(local_top, "ctx"), sink_logits[:, None])
    global_expo = jnp.exp(global_scores - global_top[..., None])
    part_total = jnp.sum(global_expo, axis=2)
    part_acc = jnp.einsum(
        "hgt,htd->hgd",
        global_expo.astype(jnp.bfloat16),
        value_heads,
        preferred_element_type=jnp.float32,
    )
    summed_total, summed_acc = lax.psum((part_total, part_acc), "ctx")
    global_total = jnp.exp(sink_logits[:, None] - global_top) + summed_total
    global_out = summed_acc / global_total[..., None]
    global_lse = global_top + jnp.log(global_total)
    row_index = jnp.arange(tokens)
    first_rows = is_first & (row_index < BLOCK)
    last_rows = is_last & (row_index >= tokens - BLOCK)
    regular_rows = jnp.logical_not(first_rows | last_rows)
    out_heads = jnp.where(
        first_rows[None, :, None],
        place_rows(global_out[:, :BLOCK], 0, tokens),
        jnp.where(
            last_rows[None, :, None],
            place_rows(global_out[:, BLOCK:], tokens - BLOCK, tokens),
            regular_out,
        ),
    )
    attention_half = out_heads.astype(jnp.bfloat16)
    lse_rows = jnp.where(
        first_rows[None, :],
        jnp.pad(global_lse[:, :BLOCK], ((0, 0), (0, tokens - BLOCK))),
        jnp.where(
            last_rows[None, :],
            jnp.pad(global_lse[:, BLOCK:], ((0, 0), (tokens - BLOCK, 0))),
            regular_lse,
        ),
    )
    grad_heads = to_heads(own_grad, head_count)
    row_delta = jnp.sum(grad_heads.astype(jnp.float32) * attention_half.astype(jnp.float32), axis=2)
    grad_regular = jnp.where(regular_rows[None, :, None], grad_heads, jnp.zeros_like(grad_heads))
    grad_blocks = grad_regular.reshape(head_count, shard_blocks, BLOCK, HD)
    delta_blocks = jnp.where(regular_rows[None, :], row_delta, 0.0).reshape(
        head_count, shard_blocks, BLOCK
    )
    lse_blocks = regular_lse.reshape(head_count, shard_blocks, BLOCK)
    probs = jnp.exp(scores - lse_blocks[..., None])
    prob_grad = jnp.einsum(
        "hnqd,hnkd->hnqk", grad_blocks, slot_values, preferred_element_type=jnp.float32
    )
    score_grad = (probs * (prob_grad - delta_blocks[..., None])).astype(jnp.bfloat16)
    prob_half = probs.astype(jnp.bfloat16)
    regular_dq = (
        jnp.einsum("hnqk,hnkd->hnqd", score_grad, slot_keys, preferred_element_type=jnp.float32)
        * scaling
    ).reshape(head_count, tokens, HD)
    slot_dk = (
        jnp.einsum("hnqk,hnqd->hnkd", score_grad, query_blocks, preferred_element_type=jnp.float32)
        * scaling
    )
    slot_dv = jnp.einsum(
        "hnqk,hnqd->hnkd", prob_half, grad_blocks, preferred_element_type=jnp.float32
    )
    slot_both = jnp.stack([slot_dk, slot_dv])
    window_lower = slot_both[:, :, :, :BLOCK].reshape(2, head_count, tokens, HD)
    window_self = slot_both[:, :, :, BLOCK : 2 * BLOCK].reshape(2, head_count, tokens, HD)
    window_upper = slot_both[:, :, :, 2 * BLOCK : 3 * BLOCK].reshape(2, head_count, tokens, HD)
    from_above = passed_along(window_lower[:, :, :BLOCK].astype(jnp.bfloat16), "ctx", -1).astype(
        jnp.float32
    )
    from_below = passed_along(window_upper[:, :, tokens - BLOCK :], "ctx", 1)
    key_pair = (
        window_self
        + jnp.concatenate([window_lower[:, :, BLOCK:], from_above], axis=2)
        + jnp.concatenate([from_below, window_upper[:, :, : tokens - BLOCK]], axis=2)
    )
    global_slots = jnp.sum(slot_both[:, :, :, 3 * BLOCK : 5 * BLOCK], axis=2)
    random_pack = (
        jnp.sum(
            slot_both[:, :, :, 5 * BLOCK :].reshape(2, head_count, shard_blocks, ROUNDS, BLOCK, HD),
            axis=2,
        )
        .transpose(2, 0, 1, 3, 4)
        .astype(jnp.bfloat16)
    )
    global_probs = jnp.exp(global_scores - global_lse[..., None])
    global_att = global_out.astype(jnp.bfloat16)
    global_delta = jnp.sum(global_grad.astype(jnp.float32) * global_att.astype(jnp.float32), axis=2)
    global_dp = jnp.einsum(
        "hgd,htd->hgt", global_grad, value_heads, preferred_element_type=jnp.float32
    )
    global_ds = (global_probs * (global_dp - global_delta[..., None])).astype(jnp.bfloat16)
    part_dq = (
        jnp.einsum("hgt,htd->hgd", global_ds, key_heads, preferred_element_type=jnp.float32)
        * scaling
    )
    owned_dk = (
        jnp.einsum("hgt,hgd->htd", global_ds, global_query, preferred_element_type=jnp.float32)
        * scaling
    )
    owned_dv = jnp.einsum(
        "hgt,hgd->htd",
        global_probs.astype(jnp.bfloat16),
        global_grad,
        preferred_element_type=jnp.float32,
    )
    key_pair = key_pair + jnp.stack([owned_dk, owned_dv])
    summed_dq, summed_slots = lax.psum((part_dq, global_slots), "ctx")
    key_pair = key_pair + is_first.astype(jnp.float32) * place_rows(
        summed_slots[:, :, :BLOCK], 0, tokens
    )
    key_pair = key_pair + is_last.astype(jnp.float32) * place_rows(
        summed_slots[:, :, BLOCK:], tokens - BLOCK, tokens
    )
    returned = jnp.stack(
        [
            return_apart(random_pack[number], xor_masks[number], bit_count)
            for number in range(ROUNDS)
        ]
    )
    block_match = (jnp.arange(shard_blocks)[None, :] == wanted[:, None]).astype(jnp.float32)
    random_add = jnp.einsum("rn,rchbd->chnbd", block_match, returned.astype(jnp.float32)).reshape(
        2, head_count, tokens, HD
    )
    key_pair = key_pair + random_add
    query_total = jnp.where(
        first_rows[None, :, None],
        place_rows(summed_dq[:, :BLOCK], 0, tokens),
        jnp.where(
            last_rows[None, :, None],
            place_rows(summed_dq[:, BLOCK:], tokens - BLOCK, tokens),
            regular_dq,
        ),
    )
    sink_part = -jnp.sum(jnp.exp(sink_logits[:, None] - lse_rows) * row_delta, axis=1)
    sink_total = lax.psum(sink_part, ("dp", "ctx"))
    sink_grad = sink_total / math.sqrt(lax.axis_size("dp") * ctx_count * tokens)
    attention = from_heads(attention_half)[None]
    query_grad = from_heads(query_total.astype(jnp.bfloat16))[None]
    key_grad = from_heads(key_pair[0].astype(jnp.bfloat16))[None]
    value_grad = from_heads(key_pair[1].astype(jnp.bfloat16))[None]
    return (attention, query_grad, key_grad, value_grad, sink_grad)


def solution(mesh):
    return jax.shard_map(
        body,
        mesh=mesh,
        in_specs=(
            P("dp", "ctx", "head"),
            P("dp", "ctx", "head"),
            P("dp", "ctx", "head"),
            P("head"),
            P(),
            P("dp", None, None),
            P("dp", "ctx", "head"),
        ),
        out_specs=(
            P("dp", "ctx", "head"),
            P("dp", "ctx", "head"),
            P("dp", "ctx", "head"),
            P("dp", "ctx", "head"),
            P("head"),
        ),
        check_vma=False,
    )
```

profile of v0, /device:TPU:0, one launch (start us, length us, event | category | flops | bytes accessed | tf_op | source)
XLA Modules:
  0.0 552.5 jit_solution(8548769882886577880)
XLA Ops:
  11.6 3.2 fusion.62
  14.8 3.2 collective-permute-start
  19.3 2.6 collective-permute-start.2
  27.2 2.6 maximum_select_fusion
  40.2 1.9 broadcast_select_fusion.10
  42.1 1.7 collective-permute-start.3
  43.8 1.9 broadcast_select_fusion.8
  46.0 1.9 broadcast_select_fusion.6
  47.9 1.7 collective-permute-start.9
  49.6 1.4 pad_maximum_fusion.14
  51.0 1.8 pad_maximum_fusion.2
  52.9 4.7 copy.136
  57.5 58.3 %all-reduce.14.cloned.1.call-done = (bf16[4,128,1024]{1,2,0:T(8,128)(2,1)}, bf16[4,128,1024]{1,2,0:T(8,128)(2,1)}) async-done(((bf16[4,128,1024]{1,2,0:T(8,128)(2,1)}, bf16[4,128,1024]{1,2,0:T(8,128)(2,1)}), (bf16[4,128,1024]{1,2,0:T(8,128)(2,1)}, bf16[4,128,1024]{1,2,0:T(8,128)(2,1)})) %all-reduce.14.cloned.1.call-update) | async-done | bytes 2097168 | tf_op jit(solution)/shard_map/psum | solution.py:21
  115.9 1.4 constant_dynamic-update-slice_fusion.1
  117.3 1.5 constant_dynamic-update-slice_fusion
  120.9 1.5 fusion.103
  122.4 14.1 %pmax.7 = f32[8,256]{1,0:T(8,128)S(1)} all-reduce(f32[8,256]{1,0:T(8,128)S(1)} %get-tuple-element.72), channel_id=1, replica_groups=mesh['dp'=2,'ctx'=8,'head'=2] {'ctx'}, use_global_device_ids=true, to_apply=%region_3.4 | all-reduce | flops 2048 | bytes 16384 | tf_op jit(solution)/shard_map/pmax | solution.py:188
  136.9 13.9 %psum.52 = f32[8,256]{1,0:T(8,128)S(1)} all-reduce(f32[8,256]{1,0:T(8,128)S(1)} %fusion.38), channel_id=1, replica_groups=mesh['dp'=2,'ctx'=8,'head'=2] {'ctx'}, use_global_device_ids=true, to_apply=%region_6.7 | all-reduce | flops 2048 | bytes 16384 | tf_op jit(solution)/shard_map/psum | solution.py:197
  150.9 1.6 fusion.47
  152.5 1.4 convolution_bitcast_fusion
  155.6 1.9 broadcast_select_fusion.9
  157.6 2.9 collective-permute-start.7
  160.4 1.9 broadcast_select_fusion.7
  162.4 47.0 %collective-permute-done.4 = bf16[128,2048]{1,0:T(8,128)(2,1)S(1)} collective-permute-done((bf16[128,2048]{1,0:T(8,128)(2,1)S(1)}, bf16[128,2048]{1,0:T(8,128)(2,1)S(1)}, u32[]{:S(2)}, u32[]{:S(2)}) %collective-permute-start.4) | collective-permute-done | bytes 524320 | tf_op jit(solution)/shard_map/ppermute | solution.py:16
  210.3 37.5 %all-reduce.10.cloned.1.call-done = f32[8,256,128]{2,1,0:T(8,128)} async-done(((f32[8,256,128]{2,1,0:T(8,128)}), f32[8,256,128]{2,1,0:T(8,128)}) %all-reduce.10.cloned.1.call-update) | async-done | bytes 1048592 | tf_op jit(solution)/shard_map/psum | solution.py:197
  247.8 1.9 multiply_reduce_fusion
  252.1 1.4 pad_maximum_fusion.11
  253.5 2.6 copy.135
  256.1 1.7 pad_maximum_fusion.3
  258.2 1.5 copy-done.6
  259.7 3.9 fusion.10
  263.6 6.5 %copy.137 = bf16[2,1024,8,128]{3,1,0,2:T(8,128)(2,1)} copy(bf16[2,1024,8,128]{1,3,2,0:T(8,128)(2,1)} %bitcast.228) | data formatting | bytes 8388608 | tf_op jit(solution)/shard_map/reshape | solution.py:142
  270.1 6.5 %copy.139 = bf16[2,1024,8,128]{3,1,0,2:T(8,128)(2,1)} copy(bf16[2,1024,8,128]{1,3,2,0:T(8,128)(2,1)} %bitcast.227) | data formatting | bytes 8388608 | tf_op jit(solution)/shard_map/reshape | solution.py:147
  276.7 3.1 bitcast_reduce_fusion
  279.8 1.9 fusion.3
  282.0 3.1 fusion.56
  285.2 1.4 fusion.51
  286.6 2.4 fusion.28
  289.0 6.9 %multiply_convert_fusion = bf16[8,2,128,1024]{2,3,1,0:T(8,128)(2,1)S(1)} fusion(f32[8,2,1024,128]{3,2,1,0:T(8,128)S(1)} %get-tuple-element.71, f32[8,2,128]{2,1,0:T(2,128)S(1)} %copy_select_fusion, f32[8,2,128]{2,1,0:T(2,128)S(1)} %get-tuple-element.26, pred[2,1024]{1,0:T(4,128)(4,1)S(1)} %add_add_fusion, bf16[8,2,128,128]{3,2,1,0:T(8,128)(2,1)S(1)} %bitcast.259, ...), kind=kOutput, calls=%fused_computation.8 | convolution fusion | flops 549453824 | bytes 17319936 | tf_op jit(solution)/shard_map/hnqd,hnkd->hnqk/dot_general | solution.py:233
  295.9 2.2 fusion.43
  299.4 2.3 fusion.5
  301.7 1.4 copy-done.1
  303.1 1.6 maximum_reduce_fusion
  304.7 5.8 %pad_maximum_fusion.6 = (f32[2,8,2,128,128]{4,3,2,1,0:T(8,128)}, f32[2,8,2,128,128]{4,3,2,1,0:T(8,128)}, f32[2,8,2,128,128]{4,3,2,1,0:T(8,128)}) fusion(f32[1,8,2,1024,128]{4,3,2,1,0:T(8,128)} %copy-done, f32[1,8,2,1024,128]{4,3,2,1,0:T(8,128)} %copy-done.1), kind=kLoop, calls=%fused_computation.40 | loop fusion | flops 1572864 | bytes 23068672 | tf_op jit(solution)/shard_map/slice | solution.py:251
  311.5 1.5 convolution_multiply_fusion.2
  313.0 57.0 %all-reduce.15 = bf16[8,256,128]{2,1,0:T(8,128)(2,1)S(1)} all-reduce(f32[8,256,128]{2,1,0:T(8,128)} %convolution_multiply_fusion.2), channel_id=1, replica_groups=mesh['dp'=2,'ctx'=8,'head'=2] {'ctx'}, use_global_device_ids=true, to_apply=%region_11.12 | all-reduce | flops 262144 | bytes 1572864 | tf_op jit(solution)/shard_map/psum | solution.py:293
  371.7 2.3 slice.260
  375.3 2.2 fusion.50
  377.4 1.6 fusion.95
  379.0 2.2 broadcast_select_fusion.4
  381.3 2.7 collective-permute-start.14
  384.8 65.5 %psum.55 = f32[8]{0:T(128)S(1)} all-reduce(f32[8]{0:T(128)S(1)} %neg.3), channel_id=1, replica_groups=mesh['dp'=2,'ctx'=8,'head'=2] {'dp','ctx'}, use_global_device_ids=true, to_apply=%region_17.18 | all-reduce | flops 8 | bytes 64 | tf_op jit(solution)/shard_map/psum | solution.py:321
  456.1 3.0 collective-permute-start.12
  460.8 1.9 broadcast_select_fusion.5
  463.3 1.9 broadcast_select_fusion.1
  465.2 2.4 collective-permute-start.21
  467.6 11.1 %collective-permute-done.17 = bf16[2,8,128,128]{3,2,1,0:T(8,128)(2,1)S(1)} collective-permute-done((bf16[2,8,128,128]{3,2,1,0:T(8,128)(2,1)}, bf16[2,8,128,128]{3,2,1,0:T(8,128)(2,1)S(1)}, u32[]{:S(2)}, u32[]{:S(2)}) %collective-permute-start.17) | collective-permute-done | bytes 524320 | tf_op jit(solution)/shard_map/ppermute | solution.py:16
  478.6 1.9 broadcast_select_fusion.3
  480.5 5.5 collective-permute-start.18
  486.1 26.5 %collective-permute-done.15 = bf16[2,8,128,128]{3,2,1,0:T(8,128)(2,1)} collective-permute-done((bf16[2,8,128,128]{3,2,1,0:T(8,128)(2,1)}, bf16[2,8,128,128]{3,2,1,0:T(8,128)(2,1)}, u32[]{:S(2)}, u32[]{:S(2)}) %collective-permute-start.15) | collective-permute-done | bytes 524320 | tf_op jit(solution)/shard_map/ppermute | solution.py:16
  514.6 9.1 %collective-permute-done.21 = bf16[2,8,128,128]{3,2,1,0:T(8,128)(2,1)} collective-permute-done((bf16[2,8,128,128]{3,2,1,0:T(8,128)(2,1)}, bf16[2,8,128,128]{3,2,1,0:T(8,128)(2,1)}, u32[]{:S(2)}, u32[]{:S(2)}) %collective-permute-start.21) | collective-permute-done | bytes 524320 | tf_op jit(solution)/shard_map/ppermute | solution.py:16
  525.9 7.2 %collective-permute-done.18 = bf16[2,8,128,128]{3,2,1,0:T(8,128)(2,1)} collective-permute-done((bf16[2,8,128,128]{3,2,1,0:T(8,128)(2,1)}, bf16[2,8,128,128]{3,2,1,0:T(8,128)(2,1)}, u32[]{:S(2)}, u32[]{:S(2)}) %collective-permute-start.18) | collective-permute-done | bytes 524320 | tf_op jit(solution)/shard_map/ppermute | solution.py:16
  535.1 4.0 fusion.41
  541.3 2.2 fusion.36
  (177 shorter events, 46.6 us)
Async XLA Ops:
  7.2 16.3 %copy-start.5 = (bf16[1,256,1024]{2,1,0:T(8,128)(2,1)S(1)}, bf16[1,256,1024]{2,1,0:T(8,128)(2,1)}, u32[]{:S(2)}) copy-start(bf16[1,256,1024]{2,1,0:T(8,128)(2,1)} %param.9) | copy-start | bytes 1572868
  7.2 17.0 %copy-start.28 = (bf16[1,256,1024]{2,1,0:T(8,128)(2,1)S(1)}, bf16[1,256,1024]{2,1,0:T(8,128)(2,1)}, u32[]{:S(2)}) copy-start(bf16[1,256,1024]{2,1,0:T(8,128)(2,1)} %param.13) | copy-start | bytes 1572868
  7.2 18.0 %copy-start.25 = (bf16[1,256,1024]{2,1,0:T(8,128)(2,1)S(1)}, bf16[1,256,1024]{2,1,0:T(8,128)(2,1)}, u32[]{:S(2)}) copy-start(bf16[1,256,1024]{2,1,0:T(8,128)(2,1)} %param.7) | copy-start | bytes 1572868
  7.2 108.7 %all-reduce.14.cloned.1.call-start = ((), (), s32[]{:S(2)}) async-start(), calls=%async_computation.2 | async-start | bytes 4194304 | tf_op jit(solution)/shard_map/psum | solution.py:21
  14.8 34.8 %collective-permute-start = (bf16[128,2048]{1,0:T(8,128)(2,1)}, bf16[128,2048]{1,0:T(8,128)(2,1)}, u32[]{:S(2)}, u32[]{:S(2)}) collective-permute-start(bf16[128,2048]{1,0:T(8,128)(2,1)} %get-tuple-element.51), channel_id=1, source_target_pairs={{0,2},{2,4},{4,6},{6,8},{8,10},{10,12},{12,14},{1,3},{3,5},{5,7},{... | collective-permute-start | bytes 1572872 | tf_op jit(solution)/shard_map/ppermute | solution.py:31
  18.0 31.7 %collective-permute-start.1 = (bf16[128,2048]{1,0:T(8,128)(2,1)}, bf16[128,2048]{1,0:T(8,128)(2,1)}, u32[]{:S(2)}, u32[]{:S(2)}) collective-permute-start(bf16[128,2048]{1,0:T(8,128)(2,1)} %get-tuple-element.52), channel_id=1, source_target_pairs={{2,0},{4,2},{6,4},{8,6},{10,8},{12,10},{14,12},{3,1},{5,3},{7,5},{... | collective-permute-start | bytes 1572872 | tf_op jit(solution)/shard_map/ppermute | solution.py:32
  19.3 20.9 %collective-permute-start.2 = (bf16[128,2048]{1,0:T(8,128)(2,1)}, bf16[128,2048]{1,0:T(8,128)(2,1)}, u32[]{:S(2)}, u32[]{:S(2)}) collective-permute-start(bf16[128,2048]{1,0:T(8,128)(2,1)} %get-tuple-element.53), channel_id=1, source_target_pairs={{0,2},{2,0},{4,6},{6,4},{8,10},{10,8},{12,14},{14,12},{1,3},{3,1},... | collective-permute-start | bytes 1572872 | tf_op jit(solution)/shard_map/ppermute | solution.py:16
  21.9 21.9 %collective-permute-start.5 = (bf16[128,2048]{1,0:T(8,128)(2,1)}, bf16[128,2048]{1,0:T(8,128)(2,1)}, u32[]{:S(2)}, u32[]{:S(2)}) collective-permute-start(bf16[128,2048]{1,0:T(8,128)(2,1)} %get-tuple-element.54), channel_id=1, source_target_pairs={{0,2},{2,0},{4,6},{6,4},{8,10},{10,8},{12,14},{14,12},{1,3},{3,1},... | collective-permute-start | bytes 1572872 | tf_op jit(solution)/shard_map/ppermute | solution.py:16
  22.0 24.1 %collective-permute-start.8 = (bf16[128,2048]{1,0:T(8,128)(2,1)}, bf16[128,2048]{1,0:T(8,128)(2,1)}, u32[]{:S(2)}, u32[]{:S(2)}) collective-permute-start(bf16[128,2048]{1,0:T(8,128)(2,1)} %get-tuple-element.55), channel_id=1, source_target_pairs={{0,2},{2,0},{4,6},{6,4},{8,10},{10,8},{12,14},{14,12},{1,3},{3,1},... | collective-permute-start | bytes 1572872 | tf_op jit(solution)/shard_map/ppermute | solution.py:16
  25.5 4.7 copy-start.31
  29.9 9.2 %copy-start.4 = (bf16[1,256,1024]{2,1,0:T(8,128)(2,1)S(1)}, bf16[1,256,1024]{2,1,0:T(8,128)(2,1)}, u32[]{:S(2)}) copy-start(bf16[1,256,1024]{2,1,0:T(8,128)(2,1)} %param.8) | copy-start | bytes 1572868
  29.9 217.9 %all-reduce.10.cloned.1.call-start = ((), (), s32[]{:S(2)}) async-start(), calls=%async_computation | async-start | bytes 2097152 | tf_op jit(solution)/shard_map/psum | solution.py:197
  39.0 111.9 %copy-start.14 = (bf16[32,8,8,128]{3,2,1,0:T(8,128)(2,1)}, bf16[32,8,8,128]{3,2,1,0:T(8,128)(2,1)S(1)}, u32[]{:S(2)}) copy-start(bf16[32,8,8,128]{3,2,1,0:T(8,128)(2,1)S(1)} %copy.195) | copy-start | bytes 1572868
  39.1 81.8 %copy-start.9 = (bf16[32,8,8,128]{3,2,1,0:T(8,128)(2,1)}, bf16[32,8,8,128]{3,2,1,0:T(8,128)(2,1)S(1)}, u32[]{:S(2)}) copy-start(bf16[32,8,8,128]{3,2,1,0:T(8,128)(2,1)S(1)} %copy.194) | copy-start | bytes 1572868
  42.1 112.3 %collective-permute-start.3 = (bf16[128,2048]{1,0:T(8,128)(2,1)}, bf16[128,2048]{1,0:T(8,128)(2,1)}, u32[]{:S(2)}, u32[]{:S(2)}) collective-permute-start(bf16[128,2048]{1,0:T(8,128)(2,1)} %broadcast_select_fusion.10), channel_id=1, source_target_pairs={{0,4},{2,6},{4,0},{6,2},{8,12},{10,14},{12,8},{14,10},{1,5},{3,7},... | collective-permute-start | bytes 1572872 | tf_op jit(solution)/shard_map/ppermute | solution.py:16
  45.7 109.9 %collective-permute-start.6 = (bf16[128,2048]{1,0:T(8,128)(2,1)}, bf16[128,2048]{1,0:T(8,128)(2,1)}, u32[]{:S(2)}, u32[]{:S(2)}) collective-permute-start(bf16[128,2048]{1,0:T(8,128)(2,1)} %broadcast_select_fusion.8), channel_id=1, source_target_pairs={{0,4},{2,6},{4,0},{6,2},{8,12},{10,14},{12,8},{14,10},{1,5},{3,7},... | collective-permute-start | bytes 1572872 | tf_op jit(solution)/shard_map/ppermute | solution.py:16
  47.9 112.5 %collective-permute-start.9 = (bf16[128,2048]{1,0:T(8,128)(2,1)}, bf16[128,2048]{1,0:T(8,128)(2,1)}, u32[]{:S(2)}, u32[]{:S(2)}) collective-permute-start(bf16[128,2048]{1,0:T(8,128)(2,1)} %broadcast_select_fusion.6), channel_id=1, source_target_pairs={{0,4},{2,6},{4,0},{6,2},{8,12},{10,14},{12,8},{14,10},{1,5},{3,7},... | collective-permute-start | bytes 1572872 | tf_op jit(solution)/shard_map/ppermute | solution.py:16
  118.7 17.8 %copy-start.29 = (f32[8]{0:T(128)S(1)}, f32[8]{0:T(128)}, u32[]{:S(2)}) copy-start(f32[8]{0:T(128)} %param.10) | copy-start | bytes 100
  119.9 1.0 copy-start.12
  122.4 30.0 %copy-start.16 = (bf16[1,256,1024]{1,2,0:T(8,128)(2,1)S(1)}, bf16[1,256,1024]{1,2,0:T(8,128)(2,1)}, u32[]{:S(2)}) copy-start(bf16[1,256,1024]{1,2,0:T(8,128)(2,1)} %get-tuple-element.38) | copy-start | bytes 1572868
  154.2 95.6 %copy-start.17 = (bf16[256,8,128]{2,0,1:T(8,128)(2,1)}, bf16[256,8,128]{2,0,1:T(8,128)(2,1)S(1)}, u32[]{:S(2)}) copy-start(bf16[256,8,128]{2,0,1:T(8,128)(2,1)S(1)} %copy.142) | copy-start | bytes 1572868
  154.2 331.8 %all-reduce.12.cloned.1.call-start = ((), (), s32[]{:S(2)}) async-start(), calls=%async_computation.1 | async-start | bytes 4194304 | tf_op jit(solution)/shard_map/psum | solution.py:293
  155.6 53.9 %collective-permute-start.4 = (bf16[128,2048]{1,0:T(8,128)(2,1)S(1)}, bf16[128,2048]{1,0:T(8,128)(2,1)S(1)}, u32[]{:S(2)}, u32[]{:S(2)}) collective-permute-start(bf16[128,2048]{1,0:T(8,128)(2,1)S(1)} %broadcast_select_fusion.11), channel_id=1, source_target_pairs={{0,8},{2,10},{4,12},{6,14},{8,0},{10,2},{12,4},{14,6},{1,9},{3,11}... | collective-permute-start | bytes 1572872 | tf_op jit(solution)/shard_map/ppermute | solution.py:16
  157.6 92.2 %collective-permute-start.7 = (bf16[128,2048]{1,0:T(8,128)(2,1)}, bf16[128,2048]{1,0:T(8,128)(2,1)}, u32[]{:S(2)}, u32[]{:S(2)}) collective-permute-start(bf16[128,2048]{1,0:T(8,128)(2,1)} %broadcast_select_fusion.9), channel_id=1, source_target_pairs={{0,8},{2,10},{4,12},{6,14},{8,0},{10,2},{12,4},{14,6},{1,9},{3,11}... | collective-permute-start | bytes 1572872 | tf_op jit(solution)/shard_map/ppermute | solution.py:16
  162.3 88.6 %collective-permute-start.10 = (bf16[128,2048]{1,0:T(8,128)(2,1)}, bf16[128,2048]{1,0:T(8,128)(2,1)}, u32[]{:S(2)}, u32[]{:S(2)}) collective-permute-start(bf16[128,2048]{1,0:T(8,128)(2,1)} %broadcast_select_fusion.7), channel_id=1, source_target_pairs={{0,8},{2,10},{4,12},{6,14},{8,0},{10,2},{12,4},{14,6},{1,9},{3,11}... | collective-permute-start | bytes 1572872 | tf_op jit(solution)/shard_map/ppermute | solution.py:16
  247.8 4.3 copy-start.26
  250.9 5.2 copy-start.27
  257.8 1.9 copy-start.6
  270.1 6.5 %copy-start.22 = (bf16[8,256,128]{2,1,0:T(8,128)(2,1)S(1)}, bf16[8,256,128]{2,1,0:T(8,128)(2,1)}, u32[]{:S(2)}) copy-start(bf16[8,256,128]{2,1,0:T(8,128)(2,1)} %copy.138) | copy-start | bytes 1572868
  279.8 2.2 copy-start.20
  282.0 3.1 copy-start.23
  282.0 3.1 copy-start.30
  282.0 4.5 copy-start.24
  289.0 12.7 %copy-start = (f32[1,8,2,1024,128]{4,3,2,1,0:T(8,128)}, f32[1,8,2,1024,128]{4,3,2,1,0:T(8,128)S(1)}, u32[]{:S(2)}) copy-start(f32[1,8,2,1024,128]{4,3,2,1,0:T(8,128)S(1)} %fusion.28) | copy-start | bytes 25165828
  289.0 6.9 %copy-start.2 = (bf16[2,1024,8,128]{3,1,0,2:T(8,128)(2,1)S(1)}, bf16[2,1024,8,128]{3,1,0,2:T(8,128)(2,1)}, u32[]{:S(2)}) copy-start(bf16[2,1024,8,128]{3,1,0,2:T(8,128)(2,1)} %copy.137) | copy-start | bytes 12582916
  299.4 3.7 copy-start.1
  304.7 5.8 %copy-start.15 = (bf16[32,8,8,128]{3,2,1,0:T(8,128)(2,1)S(1)}, bf16[32,8,8,128]{3,2,1,0:T(8,128)(2,1)}, u32[]{:S(2)}) copy-start(bf16[32,8,8,128]{3,2,1,0:T(8,128)(2,1)} %copy-done.14) | copy-start | bytes 1572868
  304.7 5.8 %copy-start.18 = (bf16[256,8,128]{2,0,1:T(8,128)(2,1)S(1)}, bf16[256,8,128]{2,0,1:T(8,128)(2,1)}, u32[]{:S(2)}) copy-start(bf16[256,8,128]{2,0,1:T(8,128)(2,1)} %copy-done.17) | copy-start | bytes 1572868
  310.4 1.0 copy-start.10
  311.5 58.5 %copy-start.3 = (bf16[2,8,384,128]{3,2,1,0:T(8,128)(2,1)S(1)}, bf16[2,8,384,128]{3,2,1,0:T(8,128)(2,1)}, u32[]{:S(2)}) copy-start(bf16[2,8,384,128]{3,2,1,0:T(8,128)(2,1)} %fusion.5) | copy-start | bytes 4718596
  371.2 7.9 %collective-permute-start.13 = (bf16[2,8,128,128]{3,2,1,0:T(8,128)(2,1)}, bf16[2,8,128,128]{3,2,1,0:T(8,128)(2,1)}, u32[]{:S(2)}, u32[]{:S(2)}) collective-permute-start(bf16[2,8,128,128]{3,2,1,0:T(8,128)(2,1)} %get-tuple-element.44), channel_id=1, source_target_pairs={{0,2},{2,0},{4,6},{6,4},{8,10},{10,8},{12,14},{14,12},{1,3},{3,1},... | collective-permute-start | bytes 1572872 | tf_op jit(solution)/shard_map/ppermute | solution.py:16
  371.2 7.9 %collective-permute-start.19 = (bf16[2,8,128,128]{3,2,1,0:T(8,128)(2,1)}, bf16[2,8,128,128]{3,2,1,0:T(8,128)(2,1)}, u32[]{:S(2)}, u32[]{:S(2)}) collective-permute-start(bf16[2,8,128,128]{3,2,1,0:T(8,128)(2,1)} %get-tuple-element.45), channel_id=1, source_target_pairs={{0,2},{2,0},{4,6},{6,4},{8,10},{10,8},{12,14},{14,12},{1,3},{3,1},... | collective-permute-start | bytes 1572872 | tf_op jit(solution)/shard_map/ppermute | solution.py:16
  371.7 7.3 %collective-permute-start.16 = (bf16[2,8,128,128]{3,2,1,0:T(8,128)(2,1)}, bf16[2,8,128,128]{3,2,1,0:T(8,128)(2,1)}, u32[]{:S(2)}, u32[]{:S(2)}) collective-permute-start(bf16[2,8,128,128]{3,2,1,0:T(8,128)(2,1)} %get-tuple-element.46), channel_id=1, source_target_pairs={{0,2},{2,0},{4,6},{6,4},{8,10},{10,8},{12,14},{14,12},{1,3},{3,1},... | collective-permute-start | bytes 1572872 | tf_op jit(solution)/shard_map/ppermute | solution.py:16
  371.7 5.7 %copy-start.7 = (f32[2,8,2,128,128]{4,3,2,1,0:T(8,128)S(1)}, f32[2,8,2,128,128]{4,3,2,1,0:T(8,128)}, u32[]{:S(2)}) copy-start(f32[2,8,2,128,128]{4,3,2,1,0:T(8,128)} %get-tuple-element.31) | copy-start | bytes 6291460
  374.0 85.7 %collective-permute-start.11 = (bf16[2,8,128,128]{3,2,1,0:T(8,128)(2,1)}, bf16[2,8,128,128]{3,2,1,0:T(8,128)(2,1)}, u32[]{:S(2)}, u32[]{:S(2)}) collective-permute-start(bf16[2,8,128,128]{3,2,1,0:T(8,128)(2,1)} %slice.260), channel_id=1, source_target_pairs={{2,0},{4,2},{6,4},{8,6},{10,8},{12,10},{14,12},{3,1},{5,3},{7,5},{... | collective-permute-start | bytes 1572872 | tf_op jit(solution)/shard_map/ppermute | solution.py:40
  377.4 6.9 %copy-start.13 = (bf16[1,256,1024]{1,2,0:T(8,128)(2,1)S(1)}, bf16[1,256,1024]{1,2,0:T(8,128)(2,1)}, u32[]{:S(2)}) copy-start(bf16[1,256,1024]{1,2,0:T(8,128)(2,1)} %copy-done.12) | copy-start | bytes 1572868
  381.3 79.6 %collective-permute-start.14 = (bf16[2,8,128,128]{3,2,1,0:T(8,128)(2,1)}, bf16[2,8,128,128]{3,2,1,0:T(8,128)(2,1)}, u32[]{:S(2)}, u32[]{:S(2)}) collective-permute-start(bf16[2,8,128,128]{3,2,1,0:T(8,128)(2,1)} %get-tuple-element.41), channel_id=1, source_target_pairs={{0,4},{2,6},{4,0},{6,2},{8,12},{10,14},{12,8},{14,10},{1,5},{3,7},... | collective-permute-start | bytes 1572872 | tf_op jit(solution)/shard_map/ppermute | solution.py:16
  384.2 79.1 %collective-permute-start.20 = (bf16[2,8,128,128]{3,2,1,0:T(8,128)(2,1)}, bf16[2,8,128,128]{3,2,1,0:T(8,128)(2,1)}, u32[]{:S(2)}, u32[]{:S(2)}) collective-permute-start(bf16[2,8,128,128]{3,2,1,0:T(8,128)(2,1)} %get-tuple-element.42), channel_id=1, source_target_pairs={{0,4},{2,6},{4,0},{6,2},{8,12},{10,14},{12,8},{14,10},{1,5},{3,7},... | collective-permute-start | bytes 1572872 | tf_op jit(solution)/shard_map/ppermute | solution.py:16
  456.1 83.3 %collective-permute-start.12 = (f32[2,8,128,128]{3,2,1,0:T(8,128)}, f32[2,8,128,128]{3,2,1,0:T(8,128)}, u32[]{:S(2)}, u32[]{:S(2)}) collective-permute-start(f32[2,8,128,128]{3,2,1,0:T(8,128)} %get-tuple-element.35), channel_id=1, source_target_pairs={{0,2},{2,4},{4,6},{6,8},{8,10},{10,12},{12,14},{1,3},{3,5},{5,7},{... | collective-permute-start | bytes 3145736 | tf_op jit(solution)/shard_map/ppermute | solution.py:40
  459.7 19.0 %collective-permute-start.17 = (bf16[2,8,128,128]{3,2,1,0:T(8,128)(2,1)}, bf16[2,8,128,128]{3,2,1,0:T(8,128)(2,1)S(1)}, u32[]{:S(2)}, u32[]{:S(2)}) collective-permute-start(bf16[2,8,128,128]{3,2,1,0:T(8,128)(2,1)} %get-tuple-element.43), channel_id=1, source_target_pairs={{0,4},{2,6},{4,0},{6,2},{8,12},{10,14},{12,8},{14,10},{1,5},{3,7},... | collective-permute-start | bytes 1572872 | tf_op jit(solution)/shard_map/ppermute | solution.py:16
  462.8 49.8 %collective-permute-start.15 = (bf16[2,8,128,128]{3,2,1,0:T(8,128)(2,1)}, bf16[2,8,128,128]{3,2,1,0:T(8,128)(2,1)}, u32[]{:S(2)}, u32[]{:S(2)}) collective-permute-start(bf16[2,8,128,128]{3,2,1,0:T(8,128)(2,1)} %broadcast_select_fusion.5), channel_id=1, source_target_pairs={{0,8},{2,10},{4,12},{6,14},{8,0},{10,2},{12,4},{14,6},{1,9},{3,11}... | collective-permute-start | bytes 1572872 | tf_op jit(solution)/shard_map/ppermute | solution.py:16
  465.2 58.6 %collective-permute-start.21 = (bf16[2,8,128,128]{3,2,1,0:T(8,128)(2,1)}, bf16[2,8,128,128]{3,2,1,0:T(8,128)(2,1)}, u32[]{:S(2)}, u32[]{:S(2)}) collective-permute-start(bf16[2,8,128,128]{3,2,1,0:T(8,128)(2,1)} %broadcast_select_fusion.1), channel_id=1, source_target_pairs={{0,8},{2,10},{4,12},{6,14},{8,0},{10,2},{12,4},{14,6},{1,9},{3,11}... | collective-permute-start | bytes 1572872 | tf_op jit(solution)/shard_map/ppermute | solution.py:16
  480.5 52.5 %collective-permute-start.18 = (bf16[2,8,128,128]{3,2,1,0:T(8,128)(2,1)}, bf16[2,8,128,128]{3,2,1,0:T(8,128)(2,1)}, u32[]{:S(2)}, u32[]{:S(2)}) collective-permute-start(bf16[2,8,128,128]{3,2,1,0:T(8,128)(2,1)} %broadcast_select_fusion.3), channel_id=1, source_target_pairs={{0,8},{2,10},{4,12},{6,14},{8,0},{10,2},{12,4},{14,6},{1,9},{3,11}... | collective-permute-start | bytes 1572872 | tf_op jit(solution)/shard_map/ppermute | solution.py:16
  535.1 4.3 copy-start.11
  535.1 4.3 copy-start.21
  539.2 1.6 copy-start.8
  539.2 1.8 slice-start
  539.2 2.2 copy-start.19
Sparse Core Ops, SparseCore 0:
  30.0 85.8 all-reduce.13
  154.3 93.4 all-reduce.9
  371.8 80.3 all-reduce.11
where the time goes:
time: 555 us; the launch traced here: 553 us
  waiting for transfers between devices  197 us (35%)
  blocking collectives  151 us (27%)
  other arithmetic  64.6 us (12%)
  local copies, waits for them, and re-layouts  57.4 us (10%)
  starting transfers between devices  30.7 us (6%)
  matrix products  29.9 us (5%)
  between operations  22.6 us (4%)
    ppermute x18, waiting for transfers between devices, partner_2(): return lax.ppermute(value, axis, pairs)  101 us
    psum x1, blocking collectives, body(): sink_total = lax.psum(sink_part, ('dp', 'ctx'))  65.5 us
    psum x1, waiting for transfers between devices, broadcast(): return lax.psum(kept, axis)  58.3 us
    psum x1, blocking collectives, body(): summed_dq, summed_slots = lax.psum((part_dq, global_slots), 'ctx')  57 us
    psum x1, waiting for transfers between devices, body(): summed_total, summed_acc = lax.psum((part_total, part_acc), 'ctx')  37.5 us
    ppermute x18, starting transfers between devices, partner_2(): return lax.ppermute(value, axis, pairs)  21.6 us
    pmax x1, blocking collectives, body(): global_top = jnp.maximum(lax.pmax(local_top, 'ctx'), sink_logits[:, None])  14.1 us
    psum x1, blocking collectives, body(): summed_total, summed_acc = lax.psum((part_total, part_acc), 'ctx')  13.9 us
  transfers between devices with their start and end apart: 25, of which 7 were waited for; matrix products, arithmetic and copies ran while one was open for 14% of the time, Pallas kernels for 0%

commit v1 on v0

v1 whole, which is shorter than its diff:
```python
import functools
import math

import jax
import jax.numpy as jnp
from jax import lax
from jax.experimental import pallas as pl
from jax.experimental.pallas import tpu as pltpu
from jax.sharding import PartitionSpec as P

HD = 128
BLOCK = 128
ROUNDS = 3
SCALE = HD ** (-0.5)
MESH = pl.DeviceIdType.MESH
F32 = jnp.float32
BF16 = jnp.bfloat16


def mm(a, b, ca, cb):
    return lax.dot_general(a, b, (((ca,), (cb,)), ((), ())), preferred_element_type=F32)


def greet(n, bit_count, me):
    barrier = pltpu.get_barrier_semaphore()
    for bit in range(bit_count):
        mask = 2**bit
        other = me + mask * (1 - 2 * ((me // mask) % 2))
        pl.semaphore_signal(barrier, inc=1, device_id={"ctx": other}, device_id_type=MESH)
    for off in (-2, -1, 1, 2):
        other = me + off

        @pl.when((other >= 0) & (other < n))
        def _():
            pl.semaphore_signal(barrier, inc=1, device_id={"ctx": other}, device_id_type=MESH)

    inside = [((me + off >= 0) & (me + off < n)).astype(jnp.int32) for off in (-2, -1, 1, 2)]
    pl.semaphore_wait(barrier, bit_count + sum(inside))


def remote(src, dst, send, recv, target):
    return pltpu.make_async_remote_copy(
        src_ref=src,
        dst_ref=dst,
        send_sem=send,
        recv_sem=recv,
        device_id={"ctx": target},
        device_id_type=MESH,
    )


def exchange_sides(n, bit_count, me, lo_src, hi_src, lo_dst, hi_dst, bit_src, bit_dst, sems):
    ws, wr, bs, br = sems

    def lower(kv):
        return remote(lo_src(kv), hi_dst(kv), ws.at[0, kv], wr.at[1, kv], me - 1)

    def upper(kv):
        return remote(hi_src(kv), lo_dst(kv), ws.at[1, kv], wr.at[0, kv], me + 1)

    def bit_copy(bit, kv):
        mask = 2**bit
        other = me + mask * (1 - 2 * ((me // mask) % 2))
        return remote(bit_src(bit, kv), bit_dst(bit, kv), bs.at[bit, kv], br.at[bit, kv], other)

    def start():
        for kv in range(2):

            @pl.when(me > 0)
            def _():
                lower(kv).start()

            @pl.when(me < n - 1)
            def _():
                upper(kv).start()

        for bit in reversed(range(bit_count)):
            for kv in range(2):
                bit_copy(bit, kv).start()

    def wait():
        for kv in range(2):

            @pl.when(me > 0)
            def _():
                lower(kv).wait_send()
                upper(kv).wait_recv()

            @pl.when(me < n - 1)
            def _():
                upper(kv).wait_send()
                lower(kv).wait_recv()

        for bit in range(bit_count):
            for kv in range(2):
                bit_copy(bit, kv).wait()

    return start, wait


def gather_kernel(
    n, bit_count, q, k, v, g, glob, win, bits, mate_s, next_s, glob_r, ws, wr, bs, br, local_s
):
    me = lax.axis_index("ctx")
    side = me % 2
    tokens = q.shape[1]
    mate = me + 1 - 2 * side
    nxt = me + 2 - 4 * side
    source = side * (n - 1)
    has_next = (nxt >= 0) & (nxt < n)
    pair = (k, v)
    greet(n, bit_count, me)

    start, wait = exchange_sides(
        n,
        bit_count,
        me,
        lambda kv: pair[kv].at[0, pl.ds(0, BLOCK)],
        lambda kv: pair[kv].at[0, pl.ds(tokens - BLOCK, BLOCK)],
        lambda kv: win.at[0, kv],
        lambda kv: win.at[1, kv],
        lambda bit, kv: pair[kv].at[0],
        lambda bit, kv: bits.at[bit, kv],
        (ws, wr, bs, br),
    )
    first_row = side * (tokens - BLOCK)

    def own_copy(j):
        ref = (q, k, v, g)[j]
        return pltpu.make_async_copy(
            ref.at[0, pl.ds(pl.multiple_of(first_row, BLOCK), BLOCK)], glob.at[side, j], local_s.at[j]
        )

    def to_mate(j, s):
        return remote(glob.at[s, j], glob.at[s, j], mate_s.at[j], glob_r.at[s, j], mate)

    def to_next(j):
        return remote(glob.at[side, j], glob.at[side, j], next_s.at[j], glob_r.at[side, j], nxt)

    order = (0, 3, 1, 2)
    is_source = me == source

    @pl.when(is_source)
    def _():
        for j in order:
            own_copy(j).start()
        for j in order:
            own_copy(j).wait()
            to_mate(j, side).start()
            to_next(j).start()

    start()

    @pl.when(jnp.logical_not(is_source))
    def _():
        for j in order:
            to_next(j).wait_recv()
            to_mate(j, side).start()

            @pl.when(has_next)
            def _():
                to_next(j).start()

    for j in order:
        to_mate(j, side).wait_send()

        @pl.when(has_next)
        def _():
            to_next(j).wait_send()

        to_mate(j, 1 - side).wait_recv()
    wait()


def return_kernel(
    n,
    bit_count,
    red,
    dwin,
    dbits,
    red_out,
    rwin,
    rbits,
    mate_buf,
    chain_buf,
    mate_s,
    mate_r,
    next_s,
    chain_r,
    ws,
    wr,
    bs,
    br,
):
    me = lax.axis_index("ctx")
    side = me % 2
    mate = me + 1 - 2 * side
    nxt = me - 2 + 4 * side
    prv = me + 2 - 4 * side
    has_next = (nxt >= 0) & (nxt < n)
    has_prev = (prv >= 0) & (prv < n)
    greet(n, bit_count, me)

    start, wait = exchange_sides(
        n,
        bit_count,
        me,
        lambda kv: dwin.at[0, kv],
        lambda kv: dwin.at[1, kv],
        lambda kv: rwin.at[0, kv],
        lambda kv: rwin.at[1, kv],
        lambda bit, kv: dbits.at[bit, kv],
        lambda bit, kv: rbits.at[bit, kv],
        (ws, wr, bs, br),
    )

    def to_mate(j):
        return remote(red.at[1 - side, j], mate_buf.at[j], mate_s.at[j], mate_r.at[j], mate)

    def to_next(j):
        return remote(red_out.at[j], chain_buf.at[j], next_s.at[j], chain_r.at[j], nxt)

    for j in range(4):
        to_mate(j).start()
    start()
    for j in range(4):
        to_mate(j).wait_recv()
        red_out[j] = (red[side, j].astype(F32) + mate_buf[j].astype(F32)).astype(BF16)

        @pl.when(has_prev)
        def _():
            to_next(j).wait_recv()
            total = red[side, j].astype(F32) + mate_buf[j].astype(F32) + chain_buf[j].astype(F32)
            red_out[j] = total.astype(BF16)

        @pl.when(has_next)
        def _():
            to_next(j).start()

    for j in range(4):
        to_mate(j).wait_send()

        @pl.when(has_next)
        def _():
            to_next(j).wait_send()

    wait()


def stats_kernel(glob, k, v, stats):
    gq = jnp.concatenate([glob[0, 0], glob[1, 0]], axis=0)
    gg = jnp.concatenate([glob[0, 3], glob[1, 3]], axis=0)
    s = mm(k[0], gq, 1, 1) * SCALE
    top = jnp.max(s, axis=0, keepdims=True)
    expo = jnp.exp(s - top)
    dp = mm(v[0], gg, 1, 1)
    stats[0, 0:1, :] = top
    stats[0, 1:2, :] = jnp.sum(expo, axis=0, keepdims=True)
    stats[0, 2:3, :] = jnp.sum(expo.astype(BF16).astype(F32) * dp, axis=0, keepdims=True)


def regular_kernel(
    info,
    sink_ref,
    q,
    k,
    v,
    g,
    win,
    glob,
    r0,
    r1,
    r2,
    att,
    dq,
    own,
    dwin,
    dglob,
    dbits,
    sink_out,
    racc,
):
    head = pl.program_id(0)
    is_first = info[6] == 1
    is_last = info[7] == 1
    sink = sink_ref[head]
    tokens = q.shape[1]
    count = tokens // BLOCK
    randoms = (r0, r1, r2)
    ext, shared = [], []
    for kv, ref in enumerate((k, v)):
        lo = jnp.where(is_first, jnp.zeros((BLOCK, HD), BF16), win[0, kv])
        hi = jnp.where(is_last, jnp.zeros((BLOCK, HD), BF16), win[1, kv])
        ext.append([lo] + [ref[0, i * BLOCK : (i + 1) * BLOCK] for i in range(count)] + [hi])
        shared.append([glob[0, 1 + kv], glob[1, 1 + kv]] + [r[0, kv] for r in randoms])
    slots = 5 + ROUNDS
    col = lax.broadcasted_iota(jnp.int32, (BLOCK, slots * BLOCK), 1)
    ext_grad = [[None] * (count + 2), [None] * (count + 2)]
    shared_grad = [None, None]
    sink_sum = jnp.zeros((1, 1), F32)
    for b in range(count):
        keys = jnp.concatenate(ext[0][b : b + 3] + shared[0], axis=0)
        vals = jnp.concatenate(ext[1][b : b + 3] + shared[1], axis=0)
        rows = slice(b * BLOCK, (b + 1) * BLOCK)
        qb, gb = q[0, rows], g[0, rows]
        s = mm(qb, keys, 1, 1) * SCALE
        if b == 1:
            s = jnp.where(is_first & (col < BLOCK), -jnp.inf, s)
        if b == count - 2:
            s = jnp.where(is_last & (col >= 2 * BLOCK) & (col < 3 * BLOCK), -jnp.inf, s)
        top = jnp.maximum(jnp.max(s, axis=1, keepdims=True), sink)
        expo = jnp.exp(s - top)
        at_sink = jnp.exp(sink - top)
        total = at_sink + jnp.sum(expo, axis=1, keepdims=True)
        inv = 1.0 / total
        out = (mm(expo.astype(BF16), vals, 1, 0) * inv).astype(BF16)
        att[rows, :] = out
        delta = jnp.sum(gb.astype(F32) * out.astype(F32), axis=1, keepdims=True)
        keep = None
        if b == 0:
            keep = jnp.logical_not(is_first)
        if b == count - 1:
            last_ok = jnp.logical_not(is_last)
            keep = last_ok if keep is None else keep & last_ok
        if keep is not None:
            inv = jnp.where(keep, inv, 0.0)
        probs = expo * inv
        dp = mm(gb, vals, 1, 1)
        ds = (probs * (dp - delta)).astype(BF16)
        ph = probs.astype(BF16)
        sink_sum = sink_sum - jnp.sum(at_sink * inv * delta, axis=0, keepdims=True)
        dq[rows, :] = (mm(ds, keys, 1, 0) * SCALE).astype(BF16)
        for kv, full in enumerate((mm(ds, qb, 0, 0) * SCALE, mm(ph, gb, 0, 0))):
            for i in range(3):
                part = full[i * BLOCK : (i + 1) * BLOCK]
                old = ext_grad[kv][b + i]
                ext_grad[kv][b + i] = part if old is None else old + part
            rest = full[3 * BLOCK :]
            shared_grad[kv] = rest if shared_grad[kv] is None else shared_grad[kv] + rest
    racc[...] = jnp.zeros_like(racc)
    for kv in range(2):
        dwin[0, kv] = ext_grad[kv][0].astype(BF16)
        dwin[1, kv] = ext_grad[kv][count + 1].astype(BF16)
        for i in range(count):
            own[kv, i * BLOCK : (i + 1) * BLOCK, :] = ext_grad[kv][i + 1]
        dglob[0, kv] = shared_grad[kv][:BLOCK].astype(BF16)
        dglob[1, kv] = shared_grad[kv][BLOCK : 2 * BLOCK].astype(BF16)
        for r in range(ROUNDS):
            at = pl.ds(pl.multiple_of(info[ROUNDS + r] * BLOCK, BLOCK), BLOCK)
            racc[info[r], kv, at, :] += shared_grad[kv][(2 + r) * BLOCK : (3 + r) * BLOCK]
    dbits[...] = racc[...].astype(BF16)
    sink_out[0] = jnp.broadcast_to(sink_sum, (8, 128))


def global_kernel(info, sink_ref, stats, glob, k, v, own, dglob, sink_in, own_out, red, sink_out):
    head = pl.program_id(0)
    sink = sink_ref[head]
    is_first = info[6] == 1
    is_last = info[7] == 1
    peers = stats.shape[0]
    gq = jnp.concatenate([glob[0, 0], glob[1, 0]], axis=0)
    gg = jnp.concatenate([glob[0, 3], glob[1, 3]], axis=0)
    tops = [stats[c, 0, 0:1, :] for c in range(peers)]
    top = functools.reduce(jnp.maximum, tops)
    top = jnp.maximum(top, sink)
    at_sink = jnp.exp(sink - top)
    total = at_sink
    delta = jnp.zeros_like(top)
    for c in range(peers):
        ratio = jnp.exp(tops[c] - top)
        total = total + stats[c, 0, 1:2, :] * ratio
        delta = delta + stats[c, 0, 2:3, :] * ratio
    inv = 1.0 / total
    delta = delta * inv
    s = mm(k[0], gq, 1, 1) * SCALE
    probs = jnp.exp(s - top) * inv
    dp = mm(v[0], gg, 1, 1)
    ds = (probs * (dp - delta)).astype(BF16)
    ph = probs.astype(BF16)
    own_out[0] = own[0] + mm(ds, gq, 1, 0) * SCALE
    own_out[1] = own[1] + mm(ph, gg, 1, 0)
    out = mm(ph, v[0], 0, 0).astype(BF16)
    gdq = (mm(ds, k[0], 0, 0) * SCALE).astype(BF16)
    for s_ in range(2):
        rows = slice(s_ * BLOCK, (s_ + 1) * BLOCK)
        red[s_, 0] = out[rows]
        red[s_, 1] = gdq[rows]
        red[s_, 2] = dglob[s_, 0]
        red[s_, 3] = dglob[s_, 1]
    terms = at_sink * inv * delta
    lane = lax.broadcasted_iota(jnp.int32, terms.shape, 1)
    mine = (is_first & (lane < BLOCK)) | (is_last & (lane >= BLOCK))
    part = jnp.sum(jnp.where(mine, terms, 0.0), axis=1, keepdims=True)
    sink_out[0] = sink_in[0] - jnp.broadcast_to(part, (8, 128))


def final_kernel(bit_count, info, att, dq, own, red, rwin, rbits, att_o, dq_o, dk_o, dv_o):
    is_first = info[6] == 1
    is_last = info[7] == 1
    tokens = att.shape[0]
    count = tokens // BLOCK
    for b in range(count):
        rows = slice(b * BLOCK, (b + 1) * BLOCK)
        a, d = att[rows, :], dq[rows, :]
        grads = [own[kv, rows, :] for kv in range(2)]
        for bit in range(bit_count):
            grads = [grads[kv] + rbits[bit, kv, rows, :].astype(F32) for kv in range(2)]
        for edge, here, side in ((0, is_first, 0), (count - 1, is_last, 1)):
            if b == edge:
                a = jnp.where(here, red[0], a)
                d = jnp.where(here, red[1], d)
                for kv in range(2):
                    grads[kv] = grads[kv] + jnp.where(here, red[2 + kv], rwin[side, kv]).astype(F32)
        att_o[0, rows, :] = a
        dq_o[0, rows, :] = d
        dk_o[0, rows, :] = grads[0].astype(BF16)
        dv_o[0, rows, :] = grads[1].astype(BF16)


def body(queries, key_rows, value_rows, sink_logits, partner, block_pick, out_grad):
    _, tokens, width = queries.shape
    heads = width // HD
    n = lax.axis_size("ctx")
    bit_count = n.bit_length() - 1
    me = lax.axis_index("ctx")
    any_spec = pl.BlockSpec(memory_space=pl.ANY)
    dma = pltpu.SemaphoreType.DMA
    masks = partner[:, 0]
    bit_of = sum(b * (jnp.right_shift(masks, b) & 1) for b in range(bit_count))
    place = jnp.bitwise_xor(me, masks)
    match = jnp.arange(n)[None, :] == place[:, None]
    del match
    wanted = block_pick[0, :, :]
    picked = jnp.sum(jnp.where(jnp.arange(n)[None, :] == me, wanted, 0), axis=1)
    flags = jnp.stack([me == 0, me == n - 1]).astype(jnp.int32)
    info = jnp.concatenate([bit_of, picked, flags]).astype(jnp.int32)
    side_sems = [dma((2, 2)), dma((2, 2)), dma((bit_count, 2)), dma((bit_count, 2))]

    def shape(dims, dtype=BF16):
        return jax.ShapeDtypeStruct(dims, dtype)

    glob, win, bits = pl.pallas_call(
        functools.partial(gather_kernel, n, bit_count),
        out_shape=(
            shape((2, 4, BLOCK, width)),
            shape((2, 2, BLOCK, width)),
            shape((bit_count, 2, tokens, width)),
        ),
        in_specs=[any_spec] * 4,
        out_specs=(any_spec,) * 3,
        scratch_shapes=[dma((4,)), dma((4,)), dma((2, 4))] + side_sems + [dma((4,))],
        compiler_params=pltpu.CompilerParams(collective_id=0, has_side_effects=True),
        name="gather_blocks",
    )(queries, key_rows, value_rows, out_grad)

    smem = pl.BlockSpec(memory_space=pltpu.SMEM)
    rows_in = pl.BlockSpec((1, tokens, HD), lambda h, *_: (0, 0, h))
    rows_out = pl.BlockSpec((tokens, HD), lambda h, *_: (0, h))
    own_spec = pl.BlockSpec((2, tokens, HD), lambda h, *_: (0, 0, h))
    glob_spec = pl.BlockSpec((2, 4, BLOCK, HD), lambda h, *_: (0, 0, 0, h))
    win_spec = pl.BlockSpec((2, 2, BLOCK, HD), lambda h, *_: (0, 0, 0, h))
    bits_spec = pl.BlockSpec((bit_count, 2, tokens, HD), lambda h, *_: (0, 0, 0, h))
    sink_spec = pl.BlockSpec((1, 8, 128), lambda h, *_: (h, 0, 0))
    stat_spec = pl.BlockSpec((1, 3, 2 * BLOCK), lambda h, *_: (h, 0, 0))
    params = pltpu.CompilerParams(vmem_limit_bytes=40 * 1024 * 1024)

    stats = pl.pallas_call(
        stats_kernel,
        grid=(heads,),
        in_specs=[glob_spec, rows_in, rows_in],
        out_specs=stat_spec,
        out_shape=shape((heads, 3, 2 * BLOCK), F32),
        compiler_params=params,
        name="global_stats",
    )(glob, key_rows, value_rows)
    all_stats = lax.all_gather(stats, "ctx")

    def random_spec(r):
        return pl.BlockSpec(
            (1, 2, BLOCK, HD), lambda h, info: (info[r], 0, info[ROUNDS + r], h)
        )

    att, dq, own, dwin, dglob, dbits, sink_part = pl.pallas_call(
        regular_kernel,
        grid_spec=pltpu.PrefetchScalarGridSpec(
            num_scalar_prefetch=1,
            grid=(heads,),
            in_specs=[smem, rows_in, rows_in, rows_in, rows_in, win_spec, glob_spec]
            + [random_spec(r) for r in range(ROUNDS)],
            out_specs=(rows_out, rows_out, own_spec, win_spec, win_spec, bits_spec, sink_spec),
            scratch_shapes=[pltpu.VMEM((bit_count, 2, tokens, HD), F32)],
        ),
        out_shape=(
            shape((tokens, width)),
            shape((tokens, width)),
            shape((2, tokens, width), F32),
            shape((2, 2, BLOCK, width)),
            shape((2, 2, BLOCK, width)),
            shape((bit_count, 2, tokens, width)),
            shape((heads, 8, 128), F32),
        ),
        compiler_params=params,
        cost_estimate=pl.CostEstimate(
            flops=4 * 10**9, bytes_accessed=2 * 10**7, transcendentals=3 * 10**6
        ),
        name="regular_rows",
    )(
        info,
        sink_logits,
        queries,
        key_rows,
        value_rows,
        out_grad,
        win,
        glob,
        bits,
        bits,
        bits,
    )

    own, red, sink_part = pl.pallas_call(
        global_kernel,
        grid_spec=pltpu.PrefetchScalarGridSpec(
            num_scalar_prefetch=1,
            grid=(heads,),
            in_specs=[
                smem,
                pl.BlockSpec((n, 1, 3, 2 * BLOCK), lambda h, *_: (0, h, 0, 0)),
                glob_spec,
                rows_in,
                rows_in,
                own_spec,
                win_spec,
                sink_spec,
            ],
            out_specs=(own_spec, glob_spec, sink_spec),
        ),
        out_shape=(
            shape((2, tokens, width), F32),
            shape((2, 4, BLOCK, width)),
            shape((heads, 8, 128), F32),
        ),
        compiler_params=params,
        name="global_rows",
    )(info, sink_logits, all_stats, glob, key_rows, value_rows, own, dglob, sink_part)

    sink_total = lax.psum(sink_part[:, 0, 0], ("dp", "ctx"))
    sink_grad = sink_total / math.sqrt(lax.axis_size("dp") * n * tokens)

    vmem = pl.BlockSpec(memory_space=pltpu.VMEM)
    red, rwin, rbits = pl.pallas_call(
        functools.partial(return_kernel, n, bit_count),
        out_shape=(
            shape((4, BLOCK, width)),
            shape((2, 2, BLOCK, width)),
            shape((bit_count, 2, tokens, width)),
        ),
        in_specs=[vmem, any_spec, any_spec],
        out_specs=(vmem, any_spec, any_spec),
        scratch_shapes=[
            pltpu.VMEM((4, BLOCK, width), BF16),
            pltpu.VMEM((4, BLOCK, width), BF16),
            dma((4,)),
            dma((4,)),
            dma((4,)),
            dma((4,)),
        ]
        + side_sems,
        compiler_params=pltpu.CompilerParams(
            collective_id=1, has_side_effects=True, vmem_limit_bytes=40 * 1024 * 1024
        ),
        name="return_blocks",
    )(red, dwin, dbits)

    final_spec = pl.BlockSpec((1, tokens, HD), lambda h, *_: (0, 0, h))
    outs = pl.pallas_call(
        functools.partial(final_kernel, bit_count),
        grid_spec=pltpu.PrefetchScalarGridSpec(
            num_scalar_prefetch=1,
            grid=(heads,),
            in_specs=[
                rows_out,
                rows_out,
                own_spec,
                pl.BlockSpec((4, BLOCK, HD), lambda h, *_: (0, 0, h)),
                win_spec,
                bits_spec,
            ],
            out_specs=(final_spec,) * 4,
        ),
        out_shape=(shape((1, tokens, width)),) * 4,
        compiler_params=params,
        name="add_up",
    )(info, att, dq, own, red, rwin, rbits)
    return (*outs, sink_grad)


def solution(mesh):
    rows = P("dp", "ctx", "head")
    return jax.shard_map(
        body,
        mesh=mesh,
        in_specs=(rows, rows, rows, P("head"), P(), P("dp", None, None), rows),
        out_specs=(rows, rows, rows, rows, P("head")),
        check_vma=False,
    )
```

time: 555 us -> 242 us (0.44)
  waiting for transfers between devices: 197 us -> 0 us
  Pallas kernels: 0 us -> 183 us
  blocking collectives: 151 us -> 47.1 us
  other arithmetic: 64.6 us -> 2.34 us
  local copies, waits for them, and re-layouts: 57.4 us -> 8 us
  starting transfers between devices: 30.7 us -> 0 us
  matrix products: 29.9 us -> 0 us
  between operations: 22.6 us -> 0.86 us
    pallas_call x0 -> x6, Pallas kernels: none -> 183 us  [the longest x1 75.1 us: body(): pl.pallas_call(functools.partial(gather_kernel, n, bit_count), out_shape=...]
    psum x3 -> x1, blocking collectives: 136 us -> 33 us  [body(): sink_total = lax.psum(sink_part[:, 0, 0], ('dp', 'ctx'))]
    ppermute x22 -> x0, waiting for transfers between devices: 101 us -> none  [the longest x18 101 us: partner_2(): return lax.ppermute(value, axis, pairs)]
    psum x3 -> x0, waiting for transfers between devices: 95.9 us -> none  [the longest x1 58.3 us: broadcast(): return lax.psum(kept, axis)]
    ppermute x22 -> x0, starting transfers between devices: 30.4 us -> none  [the longest x18 21.6 us: partner_2(): return lax.ppermute(value, axis, pairs)]
    dot_general x13 -> x0, matrix products: 29.9 us -> none  [the longest x1 6.87 us: body(): jnp.einsum('hnqd,hnkd->hnqk', grad_blocks, slot_values, preferred_element...]
    reshape x5 -> x0, local copies, waits for them, and re-layouts: 21.3 us -> none  [the longest x1 6.53 us: body(): slot_values = slot_pair[:, :, feature_width:].reshape(shard_blocks, slot_...]
    select_n x13 -> x0, other arithmetic: 21.2 us -> none  [the longest x6 10.6 us: route_apart(): jnp.where(jnp.right_shift(xor_mask, bit_place) % 2 == 1, arrived, package)]
  transfers between devices with their start and end apart: 25 -> 0, of which waited for: 7 -> 0; matrix products, arithmetic and copies ran while one was open for 14% -> 0% of each run, Pallas kernels for 0% -> 0%
where the time goes in v1:
time: 242 us
  Pallas kernels  183 us (76%)
  blocking collectives  47.1 us (19%)
  local copies, waits for them, and re-layouts  8 us (3%)
    pallas_call x1, Pallas kernels, body(): pl.pallas_call(functools.partial(gather_kernel, n, bit_count), out_shape=...  75.1 us
    pallas_call x1, Pallas kernels, body(): pl.pallas_call(functools.partial(return_kernel, n, bit_count), out_shape=...  72.1 us
    psum x1, blocking collectives, body(): sink_total = lax.psum(sink_part[:, 0, 0], ('dp', 'ctx'))  33 us
    pallas_call x1, Pallas kernels, body(): pl.pallas_call(regular_kernel, grid_spec=pltpu.PrefetchScalarGridSpec(num...  20.1 us
    all_gather x1, blocking collectives, body(): all_stats = lax.all_gather(stats, 'ctx')  14.1 us
    unnamed x36, local copies, waits for them, and re-layouts  7.71 us
    pallas_call x1, Pallas kernels, body(): pl.pallas_call(global_kernel, grid_spec=pltpu.PrefetchScalarGridSpec(num_...  7.31 us
    pallas_call x1, Pallas kernels, body(): pl.pallas_call(functools.partial(final_kernel, bit_count), grid_spec=pltp...  5.12 us

profile of v1, /device:TPU:0, one launch (start us, length us, event | category | flops | bytes accessed | tf_op | source)
XLA Modules:
  0.0 241.6 jit_solution(12145092869979685262)
XLA Ops:
  0.6 0.0 copy-start.3
  0.6 0.0 copy-start.2
  0.7 0.1 add_convert_fusion
  0.7 0.9 fusion
  1.6 0.8 add_reduce_fusion
  2.4 0.1 pad_add_fusion.info
  2.5 0.0 copy-start.14
  2.5 0.0 copy-start.15
  2.5 75.1 %gather_blocks.1 = (bf16[2,4,128,1024]{3,2,1,0:T(8,128)(2,1)}, bf16[2,2,128,1024]{3,2,1,0:T(8,128)(2,1)}, bf16[3,2,256,1024]{3,2,1,0:T(8,128)(2,1)}) custom-call(bf16[1,256,1024]{2,1,0:T(8,128)(2,1)} %q.3, bf16[1,256,1024]{2,1,0:T(8,128)(2,1)} %k.7, bf16[1,256,1024]{2,1,0:T(8,128)(2,1)} %v.7, bf16[1,256,1024]{2,1,0:T(8,128)(2,1)} %g.3), custom_call_target="tpu_custom_call" | custom-call | tf_op jit(solution)/shard_map/gather_blocks/pallas_call | solution.py:442
  77.6 0.0 copy-start.16
  77.6 0.0 copy-done.3
  77.6 0.0 copy-done.2
  77.6 0.0 copy-start
  77.6 1.6 copy-done
  79.2 0.0 copy-start.1
  79.2 0.0 copy-start.17
  79.2 3.5 %global_stats.1 = f32[8,3,256]{2,1,0:T(4,128)S(1)} custom-call(bf16[2,4,128,1024]{3,2,1,0:T(8,128)(2,1)S(1)} %copy-done, bf16[1,256,1024]{2,1,0:T(8,128)(2,1)S(1)} %copy-done.2, bf16[1,256,1024]{2,1,0:T(8,128)(2,1)S(1)} %copy-done.3), custom_call_target="tpu_custom_call" | custom-call | tf_op jit(solution)/shard_map/global_stats/pallas_call | solution.py:467
  82.7 14.1 %all-gather = f32[64,3,256]{2,0,1:T(8,128)S(1)} all-gather(f32[8,3,256]{2,0,1:T(8,128)S(1)} %copy.12), channel_id=2, replica_groups=mesh['dp'=2,'ctx'=8,'head'=2] {'ctx'}, dimensions={0}, use_global_device_ids=true | all-gather | bytes 221184 | tf_op jit(solution)/shard_map/all_gather | solution.py:476
  96.8 0.1 copy.13
  97.0 0.0 copy-done.14
  97.0 0.0 copy-done.15
  97.0 0.0 copy-done.16
  97.0 0.0 copy-done.1
  97.0 0.0 copy-done.17
  97.0 20.1 %regular_rows.1 = (bf16[256,1024]{1,0:T(8,128)(2,1)S(1)}, bf16[256,1024]{1,0:T(8,128)(2,1)S(1)}, f32[2,256,1024]{2,1,0:T(8,128)S(1)}, bf16[2,2,128,1024]{3,2,1,0...) custom-call(s32[8]{0:T(128)S(1)} %pad_add_fusion.info, ...), custom_call_target="tpu_custom_call" | custom-call | flops 4000000000 | bytes 20000000 | tf_op jit(solution)/shard_map/regular_rows/pallas_call | solution.py:483
  117.1 0.0 copy-start.4
  117.2 1.6 copy-done.4
  118.8 0.0 copy-start.8
  118.8 0.0 copy-start.10
  118.8 0.0 copy-start.12
  118.8 7.3 %global_rows.1 = (f32[2,256,1024]{2,1,0:T(8,128)S(1)}, bf16[2,4,128,1024]{3,2,1,0:T(8,128)(2,1)S(1)}, f32[8,8,128]{2,1,0:T(8,128)S(1)}) custom-call(s32[8]{0:T(128)S(1)} %pad_add_fusion.info, f32[8]{0:T(128)S(1)} %copy-done.16, f32[8,8,3,256]{3,2,1,0:T(4,128)S(1)} %bitcast.7, bf16[2,4,128,1024]{3,2,1,0:T(8,128)(2,1)S(1)} %copy-done.1, ...), custom_call_target="tpu_custom_call" | custom-call | tf_op jit(solution)/shard_map/global_rows/pallas_call | solution.py:521
  126.1 0.0 copy-done.8
  126.1 0.0 copy-done.10
  126.1 0.0 copy-done.12
  126.1 0.0 copy-start.6
  126.1 1.3 copy-done.6
  127.5 0.1 slice_reduce_fusion
  127.6 33.0 %psum.7 = f32[8]{0:T(128)S(1)} all-reduce(f32[8]{0:T(128)S(1)} %slice_reduce_fusion), channel_id=1, replica_groups=mesh['dp'=2,'ctx'=8,'head'=2] {'dp','ctx'}, use_global_device_ids=true, to_apply=%region_1.2 | all-reduce | flops 8 | bytes 64 | tf_op jit(solution)/shard_map/psum | solution.py:547
  160.6 0.5 broadcast_multiply_fusion
  161.2 0.0 copy-start.5
  161.2 1.9 copy-done.5
  163.1 0.0 copy-start.9
  163.1 1.2 copy-done.9
  164.3 0.0 copy-start.7
  164.3 0.0 copy-start.11
  164.3 0.0 copy-start.13
  164.3 72.1 %return_blocks.1 = (bf16[4,128,1024]{2,1,0:T(8,128)(2,1)S(1)}, bf16[2,2,128,1024]{3,2,1,0:T(8,128)(2,1)S(1)}, bf16[3,2,256,1024]{3,2,1,0:T(8,128)(2,1)S(1)}) custom-call(bf16[2,4,128,1024]{3,2,1,0:T(8,128)(2,1)S(1)} %get-tuple-element.34.red, bf16[2,2,128,1024]{3,2,1,0:T(8,128)(2,1)S(1)} %copy-done.9, bf16[3,2,256,1024]{3,2,1,0:T(8,128)(2,1)S(1)} %copy-done.5), custom_call_target="tpu_custom_call" | custom-call | tf_op jit(solution)/shard_map/return_blocks/pallas_call | solution.py:551
  236.4 0.0 copy-done.7
  236.4 0.0 copy-done.11
  236.5 0.0 copy-done.13
  236.5 5.1 %add_up.1 = (bf16[1,256,1024]{2,1,0:T(8,128)(2,1)}, bf16[1,256,1024]{2,1,0:T(8,128)(2,1)}, bf16[1,256,1024]{2,1,0:T(8,128)(2,1)}, bf16[1,256,1024]{2,1,0:T(8,128)(2,1)}) custom-call(s32[8]{0:T(128)S(1)} %pad_add_fusion.info, bf16[256,1024]{1,0:T(8,128)(2,1)S(1)} %copy-done.11, bf16[256,1024]{1,0:T(8,128)(2,1)S(1)} %copy-done.13, ...), custom_call_target="tpu_custom_call" | custom-call | tf_op jit(solution)/shard_map/add_up/pallas_call | solution.py:576
  (2 shorter events, 0.0 us)
Async XLA Ops:
  0.6 77.0 %copy-start.3 = (bf16[1,256,1024]{2,1,0:T(8,128)(2,1)S(1)}, bf16[1,256,1024]{2,1,0:T(8,128)(2,1)}, u32[]{:S(2)}) copy-start(bf16[1,256,1024]{2,1,0:T(8,128)(2,1)} %v.7) | copy-start | bytes 1572868
  0.6 77.0 %copy-start.2 = (bf16[1,256,1024]{2,1,0:T(8,128)(2,1)S(1)}, bf16[1,256,1024]{2,1,0:T(8,128)(2,1)}, u32[]{:S(2)}) copy-start(bf16[1,256,1024]{2,1,0:T(8,128)(2,1)} %k.7) | copy-start | bytes 1572868
  2.5 94.5 %copy-start.14 = (bf16[1,256,1024]{2,1,0:T(8,128)(2,1)S(1)}, bf16[1,256,1024]{2,1,0:T(8,128)(2,1)}, u32[]{:S(2)}) copy-start(bf16[1,256,1024]{2,1,0:T(8,128)(2,1)} %q.3) | copy-start | bytes 1572868
  2.5 94.5 %copy-start.15 = (bf16[1,256,1024]{2,1,0:T(8,128)(2,1)S(1)}, bf16[1,256,1024]{2,1,0:T(8,128)(2,1)}, u32[]{:S(2)}) copy-start(bf16[1,256,1024]{2,1,0:T(8,128)(2,1)} %g.3) | copy-start | bytes 1572868
  77.6 19.4 %copy-start.16 = (f32[8]{0:T(128)S(1)}, f32[8]{0:T(128)}, u32[]{:S(2)}) copy-start(f32[8]{0:T(128)} %sink_ref.3) | copy-start | bytes 100
  77.6 1.6 copy-start
  79.2 17.8 %copy-start.1 = (bf16[2,4,128,1024]{3,2,1,0:T(8,128)(2,1)S(1)}, bf16[2,4,128,1024]{3,2,1,0:T(8,128)(2,1)}, u32[]{:S(2)}) copy-start(bf16[2,4,128,1024]{3,2,1,0:T(8,128)(2,1)} %get-tuple-element.26.glob) | copy-start | bytes 6291460
  79.2 17.8 %copy-start.17 = (bf16[2,2,128,1024]{3,2,1,0:T(8,128)(2,1)S(1)}, bf16[2,2,128,1024]{3,2,1,0:T(8,128)(2,1)}, u32[]{:S(2)}) copy-start(bf16[2,2,128,1024]{3,2,1,0:T(8,128)(2,1)} %get-tuple-element.25.win) | copy-start | bytes 3145732
  117.1 1.6 copy-start.4
  118.8 7.3 %copy-start.8 = (bf16[2,2,128,1024]{3,2,1,0:T(8,128)(2,1)}, bf16[2,2,128,1024]{3,2,1,0:T(8,128)(2,1)S(1)}, u32[]{:S(2)}) copy-start(bf16[2,2,128,1024]{3,2,1,0:T(8,128)(2,1)S(1)} %get-tuple-element.35.dwin) | copy-start | bytes 3145732
  118.8 7.3 %copy-start.10 = (bf16[256,1024]{1,0:T(8,128)(2,1)}, bf16[256,1024]{1,0:T(8,128)(2,1)S(1)}, u32[]{:S(2)}) copy-start(bf16[256,1024]{1,0:T(8,128)(2,1)S(1)} %get-tuple-element.28.att) | copy-start | bytes 1572868
  118.8 7.3 %copy-start.12 = (bf16[256,1024]{1,0:T(8,128)(2,1)}, bf16[256,1024]{1,0:T(8,128)(2,1)S(1)}, u32[]{:S(2)}) copy-start(bf16[256,1024]{1,0:T(8,128)(2,1)S(1)} %get-tuple-element.29.dq) | copy-start | bytes 1572868
  126.1 1.3 copy-start.6
  161.2 1.9 copy-start.5
  163.1 1.2 copy-start.9
  164.3 72.2 %copy-start.7 = (f32[2,256,1024]{2,1,0:T(8,128)S(1)}, f32[2,256,1024]{2,1,0:T(8,128)}, u32[]{:S(2)}) copy-start(f32[2,256,1024]{2,1,0:T(8,128)} %copy-done.6) | copy-start | bytes 6291460
  164.3 72.2 %copy-start.11 = (bf16[256,1024]{1,0:T(8,128)(2,1)S(1)}, bf16[256,1024]{1,0:T(8,128)(2,1)}, u32[]{:S(2)}) copy-start(bf16[256,1024]{1,0:T(8,128)(2,1)} %copy-done.10) | copy-start | bytes 1572868
  164.3 72.2 %copy-start.13 = (bf16[256,1024]{1,0:T(8,128)(2,1)S(1)}, bf16[256,1024]{1,0:T(8,128)(2,1)}, u32[]{:S(2)}) copy-start(bf16[256,1024]{1,0:T(8,128)(2,1)} %copy-done.12) | copy-start | bytes 1572868
